TPU v7x, 32 devices: a whole 2x2x4 slice. The times are simulated.
32 devices in a mesh: dp: 16 (over z, y, x), tensor: 2 (over core).
Axes of the slice: x: 2, y: 2, z: 4, core: 2. Of those that a mesh axis runs over, the one named last changes fastest.
Arguments:
- tokens: float32 [16384, 768], P(('dp', 'tensor')), may hold values from -6 to 6
- offsets: int32 [16, 16], P('dp'), may hold values from 0 to 1024, as said below
- w_qkv: bfloat16 [768, 3, 768], P('dp', None, 'tensor'), may hold values from -0.21875 to 0.21875
- w_attn_out: bfloat16 [768, 768], P('tensor', 'dp'), may hold values from -1.75 to 1.75
- w_in: bfloat16 [768, 2, 1152], P('dp', None, 'tensor'), may hold values from -0.21875 to 0.21875
- w_mlp_out: bfloat16 [1152, 768], P('tensor', 'dp'), may hold values from -0.1875 to 0.1875
- gain_attn: bfloat16 [768], P('dp'), may hold values from 0.099609375 to 1.8984375
- gain_mlp: bfloat16 [768], P('dp'), may hold values from 0.099609375 to 1.8984375
- cotangent: float32 [16384, 768], P(('dp', 'tensor')), may hold values from -6 to 6
Outputs:
- outputs: float32 [16384, 768], P(('dp', 'tensor'))
- grad_tokens: float32 [16384, 768], P(('dp', 'tensor'))
- grad_w_qkv: float32 [768, 3, 768], P('dp', None, 'tensor')
- grad_w_attn_out: float32 [768, 768], P('tensor', 'dp')
- grad_w_in: float32 [768, 2, 1152], P('dp', None, 'tensor')
- grad_w_mlp_out: float32 [1152, 768], P('tensor', 'dp')
- grad_gain_attn: float32 [768], P('dp')
- grad_gain_mlp: float32 [768], P('dp')
Inputs may be any that keep to these rules, and one draw needn't show every extreme that they name: `offsets`: each row holds the first tokens of 16 sequences of one group of 1024 tokens, rising from 0 and never falling (equal entries are empty sequences); a sequence ends where the next begins, the last at 1024. No sequence has more than 512 tokens; in every row one has exactly 512 and holds the group's tokens 512 - 1 and 512.
All inputs are finite; a program needn't handle non-finite values.
Results may differ from a plain program's by a relative error of at most 0.018.
Values may be sent and summed in bfloat16 or wider, within the bound.
A program may use at most 128 MiB of HBM per device.

v0:
```python
import math
import jax
import jax.numpy as jnp
from jax import lax
from jax.sharding import PartitionSpec as P

HEAD_DIM = 64
EPSILON = 1e-05
ROPE_BASE = 160000.0
NEGATIVE = -1e30


def seq_starts(offset_row, count_rows):
    position = jnp.arange(count_rows, dtype=jnp.int32)
    before = offset_row[None, :] <= position[:, None]
    return jnp.max(jnp.where(before, offset_row[None, :], 0), axis=1)


def rope_tables(starts):
    count_rows = starts.shape[0]
    position = jnp.arange(count_rows, dtype=jnp.int32) - starts
    half_dim = HEAD_DIM // 2
    inverse = jnp.power(
        jnp.float32(ROPE_BASE), -2.0 * jnp.arange(half_dim, dtype=jnp.float32) / HEAD_DIM
    )
    angles = position.astype(jnp.float32)[:, None] * inverse[None, :]
    return (jnp.cos(angles), jnp.sin(angles))


def rotate(head_rows, cosine_tab, sine_tab):
    half_dim = HEAD_DIM // 2
    first_half = head_rows[..., :half_dim]
    second = head_rows[..., half_dim:]
    cosine_b = cosine_tab[:, None, :]
    sine_b = sine_tab[:, None, :]
    return jnp.concatenate(
        [first_half * cosine_b - second * sine_b, second * cosine_b + first_half * sine_b], axis=-1
    )


def rotate_back(head_grads, cosine_tab, sine_tab):
    half_dim = HEAD_DIM // 2
    first_half = head_grads[..., :half_dim]
    second = head_grads[..., half_dim:]
    cosine_b = cosine_tab[:, None, :]
    sine_b = sine_tab[:, None, :]
    return jnp.concatenate(
        [first_half * cosine_b + second * sine_b, second * cosine_b - first_half * sine_b], axis=-1
    )


def layer_norm(inputs_v, gain_v):
    centre = inputs_v - jnp.mean(inputs_v, axis=-1, keepdims=True)
    spread = jnp.mean(centre * centre, axis=-1, keepdims=True)
    return centre * lax.rsqrt(spread + EPSILON) * gain_v


def exact_gelu(gate_in):
    return jax.nn.gelu(gate_in, approximate=False)


def fetch_attention(w_qkv, w_attn_out, gain_attn):
    return (
        lax.all_gather(w_qkv, "dp", axis=0, tiled=True),
        lax.all_gather(w_attn_out, "dp", axis=1, tiled=True),
        lax.all_gather(gain_attn, "dp", axis=0, tiled=True),
    )


def fetch_attention_again(w_qkv, w_attn_out, gain_attn):
    return (
        lax.all_gather(w_qkv, "dp", axis=0, tiled=True),
        lax.all_gather(w_attn_out, "dp", axis=1, tiled=True),
        lax.all_gather(gain_attn, "dp", axis=0, tiled=True),
    )


def fetch_mlp(w_in, w_mlp_out, gain_mlp):
    return (
        lax.all_gather(w_in, "dp", axis=0, tiled=True),
        lax.all_gather(w_mlp_out, "dp", axis=1, tiled=True),
        lax.all_gather(gain_mlp, "dp", axis=0, tiled=True),
    )


def fetch_mlp_again(w_in, w_mlp_out, gain_mlp):
    return (
        lax.all_gather(w_in, "dp", axis=0, tiled=True),
        lax.all_gather(w_mlp_out, "dp", axis=1, tiled=True),
        lax.all_gather(gain_mlp, "dp", axis=0, tiled=True),
    )


def spread_rows(local_rows):
    return lax.all_gather(local_rows, "tensor", axis=0, tiled=True)


def spread_grads(local_rows):
    return lax.all_gather(local_rows, "tensor", axis=0, tiled=True)


def collect_rows(inputs_all, weight_full, rows_here):

    def term_of(row_start, row_count):
        return jnp.dot(inputs_all, weight_full, preferred_element_type=jnp.float32)

    return lax.psum_scatter(
        term_of(jnp.int32(0), rows_here * lax.axis_size("tensor")).astype(jnp.bfloat16),
        "tensor",
        scatter_dimension=0,
        tiled=True,
    ).astype(jnp.float32)


def collect_grads(grads_all, weight_full, rows_here):

    def term_of(row_start, row_count):
        return jnp.einsum("tsk,dsk->td", grads_all, weight_full, preferred_element_type=jnp.float32)

    return lax.psum_scatter(
        term_of(jnp.int32(0), rows_here * lax.axis_size("tensor")).astype(jnp.bfloat16),
        "tensor",
        scatter_dimension=0,
        tiled=True,
    ).astype(jnp.float32)


def block_scores(query_block, start_block, key_rows, starts, scale_factor):
    raw_scores = (
        jnp.einsum("qhe,khe->hqk", query_block, key_rows, preferred_element_type=jnp.float32)
        * scale_factor
    )
    same_seq = start_block[:, None] == starts[None, :]
    return jnp.where(same_seq[None], raw_scores, NEGATIVE)


def attention_forward(queries, key_rows, values, starts, scale_factor):
    group_rows, heads_here, head_dim = queries.shape
    block_rows = min(512, group_rows)
    block_count = group_rows // block_rows

    def one_block(block_in):
        query_block, start_block = block_in
        masked = block_scores(query_block, start_block, key_rows, starts, scale_factor)
        row_max = jnp.max(masked, axis=-1, keepdims=True)
        exp_terms = jnp.exp(masked - row_max)
        row_total = jnp.sum(exp_terms, axis=-1, keepdims=True)
        softmax_w = exp_terms / row_total
        mixed_out = jnp.einsum(
            "hqk,khe->qhe",
            softmax_w.astype(jnp.bfloat16),
            values,
            preferred_element_type=jnp.float32,
        )
        return (mixed_out, (row_max + jnp.log(row_total))[..., 0])

    mixed_all, lse_stack = lax.map(
        one_block,
        (
            queries.reshape(block_count, block_rows, heads_here, head_dim),
            starts.reshape(block_count, block_rows),
        ),
    )
    return (mixed_all.reshape(group_rows, heads_here, head_dim), lse_stack)


def attention_backward(queries, key_rows, values, starts, lse_stack, grad_out, scale_factor):
    group_rows, heads_here, head_dim = queries.shape
    block_rows = min(512, group_rows)
    block_count = group_rows // block_rows

    def one_block(carry_in, block_in):
        grad_keys, grad_values = carry_in
        query_block, start_block, lse_block, grad_block = block_in
        masked = block_scores(query_block, start_block, key_rows, starts, scale_factor)
        softmax_w = jnp.exp(masked - lse_block[..., None])
        grad_values = grad_values + jnp.einsum(
            "hqk,qhe->khe",
            softmax_w.astype(jnp.bfloat16),
            grad_block,
            preferred_element_type=jnp.float32,
        )
        grad_probs = jnp.einsum(
            "qhe,khe->hqk", grad_block, values, preferred_element_type=jnp.float32
        )
        grad_scores = softmax_w * (
            grad_probs - jnp.sum(softmax_w * grad_probs, axis=-1, keepdims=True)
        )
        rounded = grad_scores.astype(jnp.bfloat16)
        grad_query = (
            jnp.einsum("hqk,khe->qhe", rounded, key_rows, preferred_element_type=jnp.float32)
            * scale_factor
        )
        grad_keys = (
            grad_keys
            + jnp.einsum("hqk,qhe->khe", rounded, query_block, preferred_element_type=jnp.float32)
            * scale_factor
        )
        return ((grad_keys, grad_values), grad_query)

    zero_grads = jnp.zeros((group_rows, heads_here, head_dim), jnp.float32)
    block_inputs = (
        queries.reshape(block_count, block_rows, heads_here, head_dim),
        starts.reshape(block_count, block_rows),
        lse_stack,
        grad_out.reshape(block_count, block_rows, heads_here, head_dim),
    )
    (grad_keys, grad_values), grad_queries = lax.scan(
        one_block, (zero_grads, zero_grads), block_inputs
    )
    return (grad_queries.reshape(group_rows, heads_here, head_dim), grad_keys, grad_values)


def shards(tokens, offsets, w_qkv, w_attn_out, w_in, w_mlp_out, gain_attn, gain_mlp, cotangent):
    rows_here = tokens.shape[0]
    group_rows = rows_here * lax.axis_size("tensor")
    scale_factor = 1.0 / math.sqrt(HEAD_DIM)
    starts = seq_starts(offsets[0], group_rows)
    cosine_tab, sine_tab = rope_tables(starts)
    qkv_full, attn_out_full, gain_one_low = fetch_attention(w_qkv, w_attn_out, gain_attn)
    gain_one = gain_one_low.astype(jnp.float32)
    normed_all = spread_rows(layer_norm(tokens, gain_one).astype(jnp.bfloat16))
    projected = jnp.einsum("td,dsk->tsk", normed_all, qkv_full, preferred_element_type=jnp.float32)
    width_here = projected.shape[2]
    heads_here = width_here // HEAD_DIM
    split_heads = projected.reshape(group_rows, 3, heads_here, HEAD_DIM)
    queries = rotate(split_heads[:, 0], cosine_tab, sine_tab).astype(jnp.bfloat16)
    key_rows = rotate(split_heads[:, 1], cosine_tab, sine_tab).astype(jnp.bfloat16)
    values = split_heads[:, 2].astype(jnp.bfloat16)
    mixed_all, lse_stack = attention_forward(queries, key_rows, values, starts, scale_factor)
    context = mixed_all.reshape(group_rows, width_here).astype(jnp.bfloat16)
    attended = collect_rows(context, attn_out_full, rows_here)
    hidden = tokens + attended
    mlp_in_full, mlp_out_full, gain_two_low = fetch_mlp(w_in, w_mlp_out, gain_mlp)
    gain_two = gain_two_low.astype(jnp.float32)
    mlp_normed = layer_norm(hidden, gain_two).astype(jnp.bfloat16)
    mlp_in_use, mlp_out_use = (mlp_in_full, mlp_out_full)
    mlp_rows = spread_rows(mlp_normed)
    gate_up = jnp.einsum("td,dsf->tsf", mlp_rows, mlp_in_use, preferred_element_type=jnp.float32)
    gate_part = gate_up[:, 0]
    up_part = gate_up[:, 1]
    activated = exact_gelu(gate_part)
    product_rows = (activated * up_part).astype(jnp.bfloat16)
    branch = collect_rows(product_rows, mlp_out_use, rows_here)
    outputs = hidden + branch
    mlp_in_back, mlp_out_back, gain_two_again = fetch_mlp_again(w_in, w_mlp_out, gain_mlp)
    gain_two_back = gain_two_again.astype(jnp.float32)
    grad_rows = spread_grads(cotangent.astype(jnp.bfloat16))
    grad_mlp_out = jnp.einsum(
        "tf,td->fd", product_rows, grad_rows, preferred_element_type=jnp.float32
    )
    grad_product = jnp.einsum(
        "td,fd->tf", grad_rows, mlp_out_back, preferred_element_type=jnp.float32
    )
    unused_out, gelu_pull = jax.vjp(exact_gelu, gate_part)
    grad_gate = gelu_pull(grad_product * up_part)[0]
    grad_up = grad_product * activated
    grad_gate_up = jnp.stack([grad_gate, grad_up], axis=1).astype(jnp.bfloat16)
    grad_mlp_in = jnp.einsum(
        "td,tsf->dsf", mlp_rows, grad_gate_up, preferred_element_type=jnp.float32
    )
    grad_normed_two = collect_grads(grad_gate_up, mlp_in_back, rows_here)
    unused_two, norm_pull_two = jax.vjp(layer_norm, hidden, gain_two_back)
    grad_hidden_norm, grad_gain_two = norm_pull_two(grad_normed_two)
    grad_hidden = cotangent + grad_hidden_norm
    mlp_sums = (
        lax.psum_scatter(grad_mlp_in, "dp", scatter_dimension=0, tiled=True),
        lax.psum_scatter(grad_mlp_out, "dp", scatter_dimension=1, tiled=True),
        lax.psum_scatter(grad_gain_two, "dp", scatter_dimension=0, tiled=True),
    )
    qkv_back, attn_out_back, gain_one_again = fetch_attention_again(w_qkv, w_attn_out, gain_attn)
    gain_one_back = gain_one_again.astype(jnp.float32)
    grad_hidden_rows = spread_grads(grad_hidden.astype(jnp.bfloat16))
    grad_attn_out = jnp.einsum(
        "te,td->ed", context, grad_hidden_rows, preferred_element_type=jnp.float32
    )
    grad_context = jnp.einsum(
        "td,ed->te", grad_hidden_rows, attn_out_back, preferred_element_type=jnp.float32
    ).astype(jnp.bfloat16)
    grad_queries, grad_keys, grad_values = attention_backward(
        queries,
        key_rows,
        values,
        starts,
        lse_stack,
        grad_context.reshape(group_rows, heads_here, HEAD_DIM),
        scale_factor,
    )
    grad_projected = jnp.stack(
        [
            rotate_back(grad_queries, cosine_tab, sine_tab),
            rotate_back(grad_keys, cosine_tab, sine_tab),
            grad_values,
        ],
        axis=1,
    )
    grad_projected = grad_projected.reshape(group_rows, 3, width_here).astype(jnp.bfloat16)
    grad_qkv = jnp.einsum(
        "td,tsk->dsk", normed_all, grad_projected, preferred_element_type=jnp.float32
    )
    grad_normed_one = collect_grads(grad_projected, qkv_back, rows_here)
    unused_one, norm_pull_one = jax.vjp(layer_norm, tokens, gain_one_back)
    grad_tokens_norm, grad_gain_one = norm_pull_one(grad_normed_one)
    grad_tokens = grad_hidden + grad_tokens_norm
    attn_sums = (
        lax.psum_scatter(grad_qkv, "dp", scatter_dimension=0, tiled=True),
        lax.psum_scatter(grad_attn_out, "dp", scatter_dimension=1, tiled=True),
        lax.psum_scatter(grad_gain_one, "dp", scatter_dimension=0, tiled=True),
    )
    shard_mlp_in, shard_mlp_out, shard_gain_two = mlp_sums
    shard_qkv, shard_attn_out, shard_gain_one = attn_sums
    gain_one_total, gain_two_total = lax.psum((shard_gain_one, shard_gain_two), "tensor")
    return (
        outputs,
        grad_tokens,
        shard_qkv,
        shard_attn_out,
        shard_mlp_in,
        shard_mlp_out,
        gain_one_total,
        gain_two_total,
    )


def solution(mesh):
    in_specs = (
        P(("dp", "tensor"), None),
        P("dp", None),
        P("dp", None, "tensor"),
        P("tensor", "dp"),
        P("dp", None, "tensor"),
        P("tensor", "dp"),
        P("dp"),
        P("dp"),
        P(("dp", "tensor"), None),
    )
    out_specs = (
        P(("dp", "tensor"), None),
        P(("dp", "tensor"), None),
        P("dp", None, "tensor"),
        P("tensor", "dp"),
        P("dp", None, "tensor"),
        P("tensor", "dp"),
        P("dp"),
        P("dp"),
    )
    return jax.shard_map(shards, mesh=mesh, in_specs=in_specs, out_specs=out_specs, check_vma=False)
```

profile of v0, /device:TPU:0, one launch (start us, length us, event | category | flops | bytes accessed | tf_op | source)
XLA Modules:
  0.0 875.3 jit_solution(12923273058877242758)
XLA Ops:
  11.2 43.5 %all-reduce.6 = (bf16[768]{0:T(1024)(128)(2,1)S(1)}, bf16[768]{0:T(1024)(128)(2,1)S(1)}) all-reduce(bf16[768]{0:T(1024)(128)(2,1)S(1)} %dynamic-update-slice, bf16[768]{0:T(1024)(128)(2,1)S(1)} %dynamic-update-slice.1), channel_id=1, replica_groups=mesh['dp'=16,'tensor'=2] {'dp'}, use_global_device_ids=true, to_apply=%add | all-reduce | flops 1536 | bytes 6144
  57.4 41.6 %all_gather.39 = bf16[384,768]{0,1:T(8,128)(2,1)} all-gather(bf16[384,48]{0,1:T(8,128)(2,1)S(1)} %copy-done.31), channel_id=1, replica_groups=mesh['dp'=16,'tensor'=2] {'dp'}, dimensions={1}, use_global_device_ids=true | all-gather | bytes 626688 | tf_op jit(solution)/shard_map/all_gather | solution.py:65
  99.1 25.5 %all-gather.9.cloned.1.call-done = bf16[768,3,384]{2,0,1:T(8,128)(2,1)} async-done(((bf16[48,3,384]{2,0,1:T(8,128)(2,1)}), bf16[768,3,384]{2,0,1:T(8,128)(2,1)}) %all-gather.9.cloned.1.call-update) | async-done | bytes 1769488 | tf_op jit(solution)/shard_map/all_gather | solution.py:64
  132.2 25.0 %while.27 = (s32[]{:T(128)}, bf16[2,512,6,64]{1,3,2,0:T(8,128)(2,1)S(1)}, f32[2,6,512]{2,1,0:T(8,128)S(1)}, s32[2,512]{1,0:T(2,128)S(1)}, s32[1024]{0:T(1024)S(1...) while((s32[]{:T(128)}, ...), condition=%wide.region_6.7_spmd, body=%wide.region_3.6_spmd.sunk | while | flops 843576320 | bytes 42727540 | solution.py:157
  173.0 51.0 %all_gather.43 = bf16[576,768]{0,1:T(8,128)(2,1)} all-gather(bf16[576,48]{0,1:T(8,128)(2,1)S(1)} %copy-done.30), channel_id=1, replica_groups=mesh['dp'=16,'tensor'=2] {'dp'}, dimensions={1}, use_global_device_ids=true | all-gather | bytes 940032 | tf_op jit(solution)/shard_map/all_gather | solution.py:81
  226.9 20.7 %all-gather.13.cloned.1.call-done = bf16[768,2,576]{2,0,1:T(8,128)(2,1)} async-done(((bf16[48,2,576]{2,0,1:T(8,128)(2,1)}), bf16[768,2,576]{2,0,1:T(8,128)(2,1)}) %all-gather.13.cloned.1.call-update) | async-done | bytes 1769488 | tf_op jit(solution)/shard_map/all_gather | solution.py:80
  247.6 10.5 %all-gather.11.cloned.1.call-done = bf16[1024,768]{1,0:T(8,128)(2,1)} async-done(((bf16[512,768]{1,0:T(8,128)(2,1)}), bf16[1024,768]{1,0:T(8,128)(2,1)}) %all-gather.11.cloned.1.call-update) | async-done | bytes 1572880 | tf_op jit(solution)/shard_map/all_gather | solution.py:95
  277.6 7.6 reduce-scatter.13.cloned.1.call-done
  287.7 10.0 %reduce-scatter.11.cloned.1.call-done = bf16[512,768]{1,0:T(8,128)(2,1)} async-done(((bf16[1024,768]{1,0:T(8,128)(2,1)}), bf16[512,768]{1,0:T(8,128)(2,1)}) %reduce-scatter.11.cloned.1.call-update) | async-done | bytes 786448 | tf_op jit(solution)/shard_map/reduce_scatter | solution.py:107
  303.6 5.8 fusion.62
  322.7 89.6 %while.28 = (s32[]{:T(128)}, f32[1024,6,64]{0,2,1:T(8,128)S(1)}, f32[1024,6,64]{0,2,1:T(8,128)}, f32[2,512,6,64]{1,0,3,2:T(2,128)}, bf16[2,512,6,64]{1,3,2,0:T(8...) while((s32[]{:T(128)}, f32[1024,6,64]{0,2,1:T(8,128)S(1)}, ...), condition=%wide.region_16.17_spmd.clone, body=%wide.region_14.16_spmd.clone.sunk | while | flops 2063135744 | bytes 110721200 | solution.py:208
  331.6 8.4 multiply_reduce_fusion.4
  340.0 7.0 multiply_convert_fusion.6
  352.2 15.0 %dynamic_update_slice.19 = f32[2,512,6,64]{1,0,3,2:T(2,128)} dynamic-update-slice(f32[2,512,6,64]{1,0,3,2:T(2,128)} %get-tuple-element.475, f32[1,512,6,64]{1,0,3,2:T(1,128)S(1)} %copy.88, s32[]{:T(128)S(6)} %copy.108, s32[]{:T(128)} %constant.64.clone.1..sunk, s32[]{:T(128)} %constant.64.clone.1..sunk, s32[]{:T(128)} %constant.64.clone.1..sunk) | dynamic-update-slice | bytes 1572868 | tf_op jit(solution)/shard_map/while/body/jit(dynamic_update_index_in_dim)/dynamic_update_slice | solution.py:157
  370.5 6.1 bitcast_add_fusion.5
  376.5 8.5 multiply_reduce_fusion.4
  385.0 6.9 multiply_convert_fusion.6
  397.1 15.0 %dynamic_update_slice.19 = f32[2,512,6,64]{1,0,3,2:T(2,128)} dynamic-update-slice(f32[2,512,6,64]{1,0,3,2:T(2,128)} %get-tuple-element.475, f32[1,512,6,64]{1,0,3,2:T(1,128)S(1)} %copy.88, s32[]{:T(128)S(6)} %copy.108, s32[]{:T(128)} %constant.64.clone.1..sunk, s32[]{:T(128)} %constant.64.clone.1..sunk, s32[]{:T(128)} %constant.64.clone.1..sunk) | dynamic-update-slice | bytes 1572868 | tf_op jit(solution)/shard_map/while/body/jit(dynamic_update_index_in_dim)/dynamic_update_slice | solution.py:157
  440.8 16.0 %reduce-scatter.21.cloned.1.call-done = f32[48,2,576]{2,0,1:T(8,128)} async-done(((f32[768,2,576]{2,0,1:T(8,128)}), f32[48,2,576]{2,0,1:T(8,128)}) %reduce-scatter.21.cloned.1.call-update) | async-done | bytes 221200 | tf_op jit(solution)/shard_map/reduce_scatter | solution.py:267
  458.6 9.5 %reduce-scatter.15.cloned.1.call-done = bf16[512,768]{1,0:T(8,128)(2,1)} async-done(((bf16[1024,768]{1,0:T(8,128)(2,1)}), bf16[512,768]{1,0:T(8,128)(2,1)}) %reduce-scatter.15.cloned.1.call-update) | async-done | bytes 786448 | tf_op jit(solution)/shard_map/reduce_scatter | solution.py:120
  470.6 42.8 %all-reduce.4 = (f32[768]{0:T(1024)S(1)}, f32[768]{0:T(1024)S(1)}) all-reduce(f32[768]{0:T(1024)S(1)} %get-tuple-element.227, f32[768]{0:T(1024)S(1)} %copy-done.38), channel_id=10, replica_groups=mesh['dp'=16,'tensor'=2] {'dp'}, use_global_device_ids=true, to_apply=%region_25.26.clone | all-reduce | flops 1536 | bytes 12288
  520.2 80.6 %reduce-scatter.23.cloned.1.call-done = f32[576,48]{0,1:T(8,128)} async-done(((f32[576,768]{0,1:T(8,128)}), f32[576,48]{0,1:T(8,128)}) %reduce-scatter.23.cloned.1.call-update) | async-done | bytes 110608 | tf_op jit(solution)/shard_map/reduce_scatter | solution.py:268
  600.8 128.6 %reduce-scatter.19.cloned.1.call-done = f32[384,48]{0,1:T(8,128)} async-done(((f32[384,768]{0,1:T(8,128)}), f32[384,48]{0,1:T(8,128)}) %reduce-scatter.19.cloned.1.call-update) | async-done | bytes 73744 | tf_op jit(solution)/shard_map/reduce_scatter | solution.py:307
  729.4 138.9 %reduce-scatter.17.cloned.1.call-done = f32[48,3,384]{2,0,1:T(8,128)} async-done(((f32[768,3,384]{2,0,1:T(8,128)}), f32[48,3,384]{2,0,1:T(8,128)}) %reduce-scatter.17.cloned.1.call-update) | async-done | bytes 221200 | tf_op jit(solution)/shard_map/reduce_scatter | solution.py:306
  (221 shorter events, 158.7 us)
Async XLA Ops:
  7.2 91.8 %all-gather.7.cloned.1.call-start = ((), (), s32[]{:S(2)}) async-start(), calls=%async_computation.8 | async-start | bytes 2359296 | tf_op jit(solution)/shard_map/all_gather | solution.py:95
  9.1 46.8 %copy-start.28 = (f32[512]{0:T(512)}, f32[512]{0:T(512)S(1)}, u32[]{:S(2)}) copy-start(f32[512]{0:T(512)S(1)} %broadcast_multiply_fusion.1) | copy-start | bytes 6148
  9.1 47.6 %copy-start.40 = (s32[1,16]{1,0:T(1,128)S(1)}, s32[1,16]{1,0:T(1,128)}, u32[]{:S(2)}) copy-start(s32[1,16]{1,0:T(1,128)} %param.14) | copy-start | bytes 196
  9.1 48.3 %copy-start.31 = (bf16[384,48]{0,1:T(8,128)(2,1)S(1)}, bf16[384,48]{0,1:T(8,128)(2,1)}, u32[]{:S(2)}) copy-start(bf16[384,48]{0,1:T(8,128)(2,1)} %param.16) | copy-start | bytes 110596
  9.4 45.3 %copy-start.36 = (f32[512]{0:T(512)}, f32[512]{0:T(512)S(1)}, u32[]{:S(2)}) copy-start(f32[512]{0:T(512)S(1)} %multiply_reduce_fusion.2) | copy-start | bytes 6148
  9.4 47.4 %copy-start.32 = (f32[512]{0:T(512)}, f32[512]{0:T(512)S(1)}, u32[]{:S(2)}) copy-start(f32[512]{0:T(512)S(1)} %fusion.74) | copy-start | bytes 6148
  55.9 68.7 %all-gather.9.cloned.1.call-start = ((), (), s32[]{:S(2)}) async-start(), calls=%async_computation.9 | async-start | bytes 1880064 | tf_op jit(solution)/shard_map/all_gather | solution.py:64
  56.6 112.7 %reduce-scatter.9.cloned.1.call-start = ((), (), s32[]{:S(2)}) async-start(), calls=%async_computation.10 | async-start | bytes 2359296 | tf_op jit(solution)/shard_map/reduce_scatter | solution.py:107
  57.4 72.6 %copy-start.12 = (f32[1024,32]{0,1:T(8,128)}, f32[1024,32]{0,1:T(8,128)S(1)}, u32[]{:S(2)}) copy-start(f32[1024,32]{0,1:T(8,128)S(1)} %get-tuple-element.302) | copy-start | bytes 393220
  57.4 72.6 %copy-start.14 = (f32[1024,32]{0,1:T(8,128)}, f32[1024,32]{0,1:T(8,128)S(1)}, u32[]{:S(2)}) copy-start(f32[1024,32]{0,1:T(8,128)S(1)} %get-tuple-element.303) | copy-start | bytes 393220
  161.3 62.8 %all-gather.15.cloned.1.call-start = ((), (), s32[]{:S(2)}) async-start(), calls=%async_computation.14 | async-start | bytes 2359296 | tf_op jit(solution)/shard_map/all_gather | solution.py:99
  163.8 83.8 %all-gather.13.cloned.1.call-start = ((), (), s32[]{:S(2)}) async-start(), calls=%async_computation.12 | async-start | bytes 2088960 | tf_op jit(solution)/shard_map/all_gather | solution.py:80
  164.5 93.6 %all-gather.11.cloned.1.call-start = ((), (), s32[]{:S(2)}) async-start(), calls=%async_computation.11 | async-start | bytes 2359296 | tf_op jit(solution)/shard_map/all_gather | solution.py:95
  173.0 112.2 %reduce-scatter.13.cloned.1.call-start = ((), (), s32[]{:S(2)}) async-start(), calls=%async_computation.15 | async-start | bytes 2359296 | tf_op jit(solution)/shard_map/reduce_scatter | solution.py:120
  274.8 22.9 %reduce-scatter.11.cloned.1.call-start = ((), (), s32[]{:S(2)}) async-start(), calls=%async_computation.13 | async-start | bytes 2359296 | tf_op jit(solution)/shard_map/reduce_scatter | solution.py:107
  277.6 36.7 %all-gather.17.cloned.1.call-start = ((), (), s32[]{:S(2)}) async-start(), calls=%async_computation.16 | async-start | bytes 2359296 | tf_op jit(solution)/shard_map/all_gather | solution.py:99
  303.1 153.7 %reduce-scatter.21.cloned.1.call-start = ((), (), s32[]{:S(2)}) async-start(), calls=%async_computation.20 | async-start | bytes 4177920 | tf_op jit(solution)/shard_map/reduce_scatter | solution.py:267
  309.4 158.6 %reduce-scatter.15.cloned.1.call-start = ((), (), s32[]{:S(2)}) async-start(), calls=%async_computation.17 | async-start | bytes 2359296 | tf_op jit(solution)/shard_map/reduce_scatter | solution.py:120
  426.6 174.3 %reduce-scatter.23.cloned.1.call-start = ((), (), s32[]{:S(2)}) async-start(), calls=%async_computation.21 | async-start | bytes 2088960 | tf_op jit(solution)/shard_map/reduce_scatter | solution.py:268
  430.9 298.5 %reduce-scatter.19.cloned.1.call-start = ((), (), s32[]{:S(2)}) async-start(), calls=%async_computation.19 | async-start | bytes 1253376 | tf_op jit(solution)/shard_map/reduce_scatter | solution.py:307
  434.6 433.8 %reduce-scatter.17.cloned.1.call-start = ((), (), s32[]{:S(2)}) async-start(), calls=%async_computation.18 | async-start | bytes 3760128 | tf_op jit(solution)/shard_map/reduce_scatter | solution.py:306
  440.0 29.6 %copy-start.37 = (f32[512]{0:T(512)S(1)}, f32[512]{0:T(512)}, u32[]{:S(2)}) copy-start(f32[512]{0:T(512)} %copy-done.36) | copy-start | bytes 6148
  440.1 29.6 %copy-start.33 = (f32[512]{0:T(512)S(1)}, f32[512]{0:T(512)}, u32[]{:S(2)}) copy-start(f32[512]{0:T(512)} %copy-done.32) | copy-start | bytes 6148
  458.6 57.9 %copy-start.35 = (f32[512]{0:T(512)S(1)}, f32[512]{0:T(512)}, u32[]{:S(2)}) copy-start(f32[512]{0:T(512)} %copy-done.34) | copy-start | bytes 6148
  (34 other events, 196.8 us)
Sparse Core Ops, SparseCore 0:
  56.0 5.6 all-gather.6
  64.4 60.1 all-gather.8
  161.4 7.8 reduce-scatter.8
  170.8 10.9 all-gather.14
  185.3 62.2 all-gather.12
  249.7 8.4 all-gather.10
  274.9 10.2 reduce-scatter.12
  287.4 10.2 reduce-scatter.10
  303.3 10.9 all-gather.16
  320.1 136.6 reduce-scatter.20
  459.7 8.2 reduce-scatter.14
  473.3 127.4 reduce-scatter.22
  606.9 122.5 reduce-scatter.18
  735.8 132.5 reduce-scatter.16
where the time goes:
time: 888 us; the launch traced here: 875 us
  waiting for transfers between devices  458 us (52%)
  blocking collectives  182 us (20%)
  matrix products  107 us (12%)
  other arithmetic  56.4 us (6%)
  local copies, waits for them, and re-layouts  54.4 us (6%)
  between operations  16.3 us (2%)
    reduce_scatter x1, waiting for transfers between devices, shards(): lax.psum_scatter(grad_qkv, 'dp', scatter_dimension=0, tiled=True)  139 us
    reduce_scatter x1, waiting for transfers between devices, shards(): lax.psum_scatter(grad_attn_out, 'dp', scatter_dimension=1, tiled=True)  129 us
    unnamed x2, blocking collectives  86.3 us
    reduce_scatter x1, waiting for transfers between devices, shards(): lax.psum_scatter(grad_mlp_out, 'dp', scatter_dimension=1, tiled=True)  80.6 us
    all_gather x1, blocking collectives, fetch_mlp(): lax.all_gather(w_mlp_out, 'dp', axis=1, tiled=True)  51 us
    all_gather x1, blocking collectives, fetch_attention(): lax.all_gather(w_attn_out, 'dp', axis=1, tiled=True)  41.6 us
    dynamic_update_slice x4, local copies, waits for them, and re-layouts, attention_forward(): lax.map(one_block, (queries.reshape(block_count, block_rows, heads_here,...  31.7 us
    all_gather x1, waiting for transfers between devices, fetch_attention(): lax.all_gather(w_qkv, 'dp', axis=0, tiled=True)  25.5 us
  transfers between devices with their start and end apart: 14, of which 12 were waited for; matrix products, arithmetic and copies ran while one was open for 18% of the time, Pallas kernels for 0%

commit v1 on v0

--- a/solution.py
+++ b/solution.py
@@ -60,9 +60,23 @@
 
 
 def fetch_attention(w_qkv, w_attn_out, gain_attn):
+
+    def time_the_face(local_block):
+        w_next, newest = (jax.lax.axis_size("dp"), jax.lax.axis_index("dp"))
+        found_now, small = (local_block, 1)
+        while small < w_next:
+            block_out = jax.lax.ppermute(
+                found_now, axis_name="dp", perm=tuple(((rr, rr ^ small) for rr in range(w_next)))
+            )
+            wide_out = jnp.concatenate([found_now, block_out], axis=1)
+            arr_out = jnp.concatenate([block_out, found_now], axis=1)
+            found_now = jnp.where(newest & small == 0, wide_out, arr_out)
+            small = 2 * small
+        return found_now
+
     return (
         lax.all_gather(w_qkv, "dp", axis=0, tiled=True),
-        lax.all_gather(w_attn_out, "dp", axis=1, tiled=True),
+        time_the_face(w_attn_out),
         lax.all_gather(gain_attn, "dp", axis=0, tiled=True),
     )
 

time: 888 us -> 920 us (1.036)
  waiting for transfers between devices: 458 us -> 482 us
    all_gather x1, waiting for transfers between devices: 25.5 us -> 52.5 us  [fetch_attention(): lax.all_gather(w_qkv, 'dp', axis=0, tiled=True)]
    ppermute x0 -> x4, waiting for transfers between devices: none -> 14.2 us  [time_the_face(): jax.lax.ppermute(found_now, axis_name='dp', perm=tuple(((rr, rr ^ small)...]
    reduce_scatter x1, waiting for transfers between devices: 16 us -> 4.33 us  [shards(): lax.psum_scatter(grad_mlp_in, 'dp', scatter_dimension=0, tiled=True)]
  transfers between devices with their start and end apart: 14 -> 18, of which waited for: 12 -> 14; matrix products, arithmetic and copies ran while one was open for 18% -> 21% of each run, Pallas kernels for 0% -> 0%
where the time goes in v1:
time: 920 us; the launch traced here: 907 us
  waiting for transfers between devices  482 us (52%)
  blocking collectives  187 us (20%)
  matrix products  108 us (12%)
  other arithmetic  57.3 us (6%)
  local copies, waits for them, and re-layouts  54.7 us (6%)
  between operations  16.4 us (2%)
    reduce_scatter x1, waiting for transfers between devices, shards(): lax.psum_scatter(grad_qkv, 'dp', scatter_dimension=0, tiled=True)  139 us
    reduce_scatter x1, waiting for transfers between devices, shards(): lax.psum_scatter(grad_attn_out, 'dp', scatter_dimension=1, tiled=True)  129 us
    unnamed x2, blocking collectives  86.2 us
    reduce_scatter x1, waiting for transfers between devices, shards(): lax.psum_scatter(grad_mlp_out, 'dp', scatter_dimension=1, tiled=True)  80.4 us
    all_gather x1, waiting for transfers between devices, fetch_attention(): lax.all_gather(w_qkv, 'dp', axis=0, tiled=True)  52.5 us
    all_gather x1, blocking collectives, fetch_mlp(): lax.all_gather(w_mlp_out, 'dp', axis=1, tiled=True)  51.2 us
    all_gather x1, blocking collectives, fetch_attention_again(): lax.all_gather(w_attn_out, 'dp', axis=1, tiled=True)  46.6 us
    dynamic_update_slice x4, local copies, waits for them, and re-layouts, attention_forward(): lax.map(one_block, (queries.reshape(block_count, block_rows, heads_here,...  31.5 us
  transfers between devices with their start and end apart: 18, of which 14 were waited for; matrix products, arithmetic and copies ran while one was open for 21% of the time, Pallas kernels for 0%

profile of v1, /device:TPU:0, one launch (start us, length us, event | category | flops | bytes accessed | tf_op | source)
XLA Modules:
  0.0 907.4 jit_solution(3288039659741372132)
XLA Ops:
  11.2 43.5 %all-reduce.6 = (bf16[768]{0:T(1024)(128)(2,1)S(1)}, bf16[768]{0:T(1024)(128)(2,1)S(1)}) all-reduce(bf16[768]{0:T(1024)(128)(2,1)S(1)} %dynamic-update-slice, bf16[768]{0:T(1024)(128)(2,1)S(1)} %dynamic-update-slice.1), channel_id=1, replica_groups=mesh['dp'=16,'tensor'=2] {'dp'}, use_global_device_ids=true, to_apply=%add | all-reduce | flops 1536 | bytes 6144
  65.8 6.1 collective-permute-done.2
  72.7 52.5 %all-gather.9.cloned.1.call-done = bf16[768,3,384]{2,0,1:T(8,128)(2,1)} async-done(((bf16[48,3,384]{2,0,1:T(8,128)(2,1)}), bf16[768,3,384]{2,0,1:T(8,128)(2,1)}) %all-gather.9.cloned.1.call-update) | async-done | bytes 1769488 | tf_op jit(solution)/shard_map/all_gather | solution.py:78
  132.8 25.0 %while.27 = (s32[]{:T(128)}, bf16[2,512,6,64]{1,3,2,0:T(8,128)(2,1)S(1)}, f32[2,6,512]{2,1,0:T(8,128)S(1)}, s32[2,512]{1,0:T(2,128)S(1)}, s32[1024]{0:T(1024)S(1...) while((s32[]{:T(128)}, ...), condition=%wide.region_6.7_spmd, body=%wide.region_3.6_spmd.sunk | while | flops 843576320 | bytes 42727540 | solution.py:171
  175.0 51.2 %all_gather.41 = bf16[576,768]{0,1:T(8,128)(2,1)} all-gather(bf16[576,48]{0,1:T(8,128)(2,1)S(1)} %copy-done.30), channel_id=1, replica_groups=mesh['dp'=16,'tensor'=2] {'dp'}, dimensions={1}, use_global_device_ids=true | all-gather | bytes 940032 | tf_op jit(solution)/shard_map/all_gather | solution.py:95
  229.0 20.2 %all-gather.13.cloned.1.call-done = bf16[768,2,576]{2,0,1:T(8,128)(2,1)} async-done(((bf16[48,2,576]{2,0,1:T(8,128)(2,1)}), bf16[768,2,576]{2,0,1:T(8,128)(2,1)}) %all-gather.13.cloned.1.call-update) | async-done | bytes 1769488 | tf_op jit(solution)/shard_map/all_gather | solution.py:94
  249.2 10.5 %all-gather.11.cloned.1.call-done = bf16[1024,768]{1,0:T(8,128)(2,1)} async-done(((bf16[512,768]{1,0:T(8,128)(2,1)}), bf16[1024,768]{1,0:T(8,128)(2,1)}) %all-gather.11.cloned.1.call-update) | async-done | bytes 1572880 | tf_op jit(solution)/shard_map/all_gather | solution.py:109
  279.2 7.6 reduce-scatter.13.cloned.1.call-done
  289.3 10.0 %reduce-scatter.11.cloned.1.call-done = bf16[512,768]{1,0:T(8,128)(2,1)} async-done(((bf16[1024,768]{1,0:T(8,128)(2,1)}), bf16[512,768]{1,0:T(8,128)(2,1)}) %reduce-scatter.11.cloned.1.call-update) | async-done | bytes 786448 | tf_op jit(solution)/shard_map/reduce_scatter | solution.py:121
  304.8 46.6 %all_gather.44 = bf16[384,768]{0,1:T(8,128)(2,1)} all-gather(bf16[384,48]{0,1:T(8,128)(2,1)} %param.16), channel_id=1, replica_groups=mesh['dp'=16,'tensor'=2] {'dp'}, dimensions={1}, use_global_device_ids=true | all-gather | bytes 626688 | tf_op jit(solution)/shard_map/all_gather | solution.py:87
  351.4 5.8 fusion.62
  366.7 89.5 %while.28 = (s32[]{:T(128)}, f32[1024,6,64]{0,2,1:T(8,128)S(1)}, f32[1024,6,64]{0,2,1:T(8,128)}, f32[2,512,6,64]{1,0,3,2:T(2,128)}, bf16[2,512,6,64]{1,3,2,0:T(8...) while((s32[]{:T(128)}, f32[1024,6,64]{0,2,1:T(8,128)S(1)}, ...), condition=%wide.region_16.17_spmd.clone, body=%wide.region_14.16_spmd.clone.sunk | while | flops 2063135744 | bytes 110721200 | solution.py:222
  375.6 8.5 multiply_reduce_fusion.4
  384.1 7.0 multiply_convert_fusion.6
  396.3 14.9 %dynamic_update_slice.19 = f32[2,512,6,64]{1,0,3,2:T(2,128)} dynamic-update-slice(f32[2,512,6,64]{1,0,3,2:T(2,128)} %get-tuple-element.475, f32[1,512,6,64]{1,0,3,2:T(1,128)S(1)} %copy.88, s32[]{:T(128)S(6)} %copy.108, s32[]{:T(128)} %constant.70.clone.1..sunk, s32[]{:T(128)} %constant.70.clone.1..sunk, s32[]{:T(128)} %constant.70.clone.1..sunk) | dynamic-update-slice | bytes 1572868 | tf_op jit(solution)/shard_map/while/body/jit(dynamic_update_index_in_dim)/dynamic_update_slice | solution.py:171
  414.4 6.1 bitcast_add_fusion.5
  420.5 8.5 multiply_reduce_fusion.4
  429.0 6.9 multiply_convert_fusion.6
  441.1 15.0 %dynamic_update_slice.19 = f32[2,512,6,64]{1,0,3,2:T(2,128)} dynamic-update-slice(f32[2,512,6,64]{1,0,3,2:T(2,128)} %get-tuple-element.475, f32[1,512,6,64]{1,0,3,2:T(1,128)S(1)} %copy.88, s32[]{:T(128)S(6)} %copy.108, s32[]{:T(128)} %constant.70.clone.1..sunk, s32[]{:T(128)} %constant.70.clone.1..sunk, s32[]{:T(128)} %constant.70.clone.1..sunk) | dynamic-update-slice | bytes 1572868 | tf_op jit(solution)/shard_map/while/body/jit(dynamic_update_index_in_dim)/dynamic_update_slice | solution.py:171
  490.8 9.5 %reduce-scatter.15.cloned.1.call-done = bf16[512,768]{1,0:T(8,128)(2,1)} async-done(((bf16[1024,768]{1,0:T(8,128)(2,1)}), bf16[512,768]{1,0:T(8,128)(2,1)}) %reduce-scatter.15.cloned.1.call-update) | async-done | bytes 786448 | tf_op jit(solution)/shard_map/reduce_scatter | solution.py:134
  502.8 42.7 %all-reduce.4 = (f32[768]{0:T(1024)S(1)}, f32[768]{0:T(1024)S(1)}) all-reduce(f32[768]{0:T(1024)S(1)} %get-tuple-element.227, f32[768]{0:T(1024)S(1)} %copy-done.37), channel_id=10, replica_groups=mesh['dp'=16,'tensor'=2] {'dp'}, use_global_device_ids=true, to_apply=%region_25.26.clone | all-reduce | flops 1536 | bytes 12288
  552.4 80.4 %reduce-scatter.23.cloned.1.call-done = f32[576,48]{0,1:T(8,128)} async-done(((f32[576,768]{0,1:T(8,128)}), f32[576,48]{0,1:T(8,128)}) %reduce-scatter.23.cloned.1.call-update) | async-done | bytes 110608 | tf_op jit(solution)/shard_map/reduce_scatter | solution.py:282
  632.8 128.6 %reduce-scatter.19.cloned.1.call-done = f32[384,48]{0,1:T(8,128)} async-done(((f32[384,768]{0,1:T(8,128)}), f32[384,48]{0,1:T(8,128)}) %reduce-scatter.19.cloned.1.call-update) | async-done | bytes 73744 | tf_op jit(solution)/shard_map/reduce_scatter | solution.py:321
  761.4 139.1 %reduce-scatter.17.cloned.1.call-done = f32[48,3,384]{2,0,1:T(8,128)} async-done(((f32[768,3,384]{2,0,1:T(8,128)}), f32[48,3,384]{2,0,1:T(8,128)}) %reduce-scatter.17.cloned.1.call-update) | async-done | bytes 221200 | tf_op jit(solution)/shard_map/reduce_scatter | solution.py:320
  (230 shorter events, 169.3 us)
Async XLA Ops:
  7.2 65.5 %all-gather.7.cloned.1.call-start = ((), (), s32[]{:S(2)}) async-start(), calls=%async_computation.8 | async-start | bytes 2359296 | tf_op jit(solution)/shard_map/all_gather | solution.py:109
  9.1 47.7 %copy-start.39 = (s32[1,16]{1,0:T(1,128)S(1)}, s32[1,16]{1,0:T(1,128)}, u32[]{:S(2)}) copy-start(s32[1,16]{1,0:T(1,128)} %param.14) | copy-start | bytes 196
  9.4 55.8 %copy-start.31 = (f32[512]{0:T(512)}, f32[512]{0:T(512)S(1)}, u32[]{:S(2)}) copy-start(f32[512]{0:T(512)S(1)} %fusion.80) | copy-start | bytes 6148
  55.9 69.4 %all-gather.9.cloned.1.call-start = ((), (), s32[]{:S(2)}) async-start(), calls=%async_computation.9 | async-start | bytes 1880064 | tf_op jit(solution)/shard_map/all_gather | solution.py:78
  56.6 114.6 %reduce-scatter.9.cloned.1.call-start = ((), (), s32[]{:S(2)}) async-start(), calls=%async_computation.10 | async-start | bytes 2359296 | tf_op jit(solution)/shard_map/reduce_scatter | solution.py:121
  56.7 4.0 collective-permute-start
  60.7 4.4 collective-permute-start.1
  65.2 6.8 collective-permute-start.2
  65.8 64.9 %copy-start.12 = (f32[1024,32]{0,1:T(8,128)}, f32[1024,32]{0,1:T(8,128)S(1)}, u32[]{:S(2)}) copy-start(f32[1024,32]{0,1:T(8,128)S(1)} %get-tuple-element.302) | copy-start | bytes 393220
  65.8 64.9 %copy-start.14 = (f32[1024,32]{0,1:T(8,128)}, f32[1024,32]{0,1:T(8,128)S(1)}, u32[]{:S(2)}) copy-start(f32[1024,32]{0,1:T(8,128)S(1)} %get-tuple-element.303) | copy-start | bytes 393220
  72.7 86.1 %collective-permute-start.3 = (bf16[384,384]{0,1:T(8,128)(2,1)}, bf16[384,384]{0,1:T(8,128)(2,1)}, u32[]{:S(2)}, u32[]{:S(2)}) collective-permute-start(bf16[384,384]{0,1:T(8,128)(2,1)} %maximum_select_fusion.2), channel_id=1, source_target_pairs={{0,16},{2,18},{4,20},{6,22},{8,24},{10,26},{12,28},{14,30},{16,0},... | collective-permute-start | bytes 884744 | tf_op jit(solution)/shard_map/ppermute | solution.py:68
  163.3 62.9 %all-gather.15.cloned.1.call-start = ((), (), s32[]{:S(2)}) async-start(), calls=%async_computation.14 | async-start | bytes 2359296 | tf_op jit(solution)/shard_map/all_gather | solution.py:113
  165.7 83.5 %all-gather.13.cloned.1.call-start = ((), (), s32[]{:S(2)}) async-start(), calls=%async_computation.12 | async-start | bytes 2088960 | tf_op jit(solution)/shard_map/all_gather | solution.py:94
  166.5 93.3 %all-gather.11.cloned.1.call-start = ((), (), s32[]{:S(2)}) async-start(), calls=%async_computation.11 | async-start | bytes 2359296 | tf_op jit(solution)/shard_map/all_gather | solution.py:109
  174.9 111.8 %reduce-scatter.13.cloned.1.call-start = ((), (), s32[]{:S(2)}) async-start(), calls=%async_computation.15 | async-start | bytes 2359296 | tf_op jit(solution)/shard_map/reduce_scatter | solution.py:134
  276.4 22.9 %reduce-scatter.11.cloned.1.call-start = ((), (), s32[]{:S(2)}) async-start(), calls=%async_computation.13 | async-start | bytes 2359296 | tf_op jit(solution)/shard_map/reduce_scatter | solution.py:121
  279.1 78.2 %all-gather.17.cloned.1.call-start = ((), (), s32[]{:S(2)}) async-start(), calls=%async_computation.16 | async-start | bytes 2359296 | tf_op jit(solution)/shard_map/all_gather | solution.py:113
  303.6 47.9 %copy-start.11 = (bf16[1024,1,576]{0,2,1:T(8,128)(2,1)S(1)}, bf16[1024,1,576]{0,2,1:T(8,128)(2,1)}, u32[]{:S(2)}) copy-start(bf16[1024,1,576]{0,2,1:T(8,128)(2,1)} %copy-done.10) | copy-start | bytes 3538948
  304.7 184.3 %reduce-scatter.21.cloned.1.call-start = ((), (), s32[]{:S(2)}) async-start(), calls=%async_computation.20 | async-start | bytes 4177920 | tf_op jit(solution)/shard_map/reduce_scatter | solution.py:281
  357.3 143.0 %reduce-scatter.15.cloned.1.call-start = ((), (), s32[]{:S(2)}) async-start(), calls=%async_computation.17 | async-start | bytes 2359296 | tf_op jit(solution)/shard_map/reduce_scatter | solution.py:134
  470.4 162.3 %reduce-scatter.23.cloned.1.call-start = ((), (), s32[]{:S(2)}) async-start(), calls=%async_computation.21 | async-start | bytes 2088960 | tf_op jit(solution)/shard_map/reduce_scatter | solution.py:282
  474.8 286.6 %reduce-scatter.19.cloned.1.call-start = ((), (), s32[]{:S(2)}) async-start(), calls=%async_computation.19 | async-start | bytes 1253376 | tf_op jit(solution)/shard_map/reduce_scatter | solution.py:321
  478.4 422.0 %reduce-scatter.17.cloned.1.call-start = ((), (), s32[]{:S(2)}) async-start(), calls=%async_computation.18 | async-start | bytes 3760128 | tf_op jit(solution)/shard_map/reduce_scatter | solution.py:320
  490.8 57.9 %copy-start.34 = (f32[512]{0:T(512)S(1)}, f32[512]{0:T(512)}, u32[]{:S(2)}) copy-start(f32[512]{0:T(512)} %copy-done.33) | copy-start | bytes 6148
  (37 other events, 339.9 us)
Sparse Core Ops, SparseCore 0:
  56.0 5.6 all-gather.6
  64.4 60.8 all-gather.8
  163.4 7.8 reduce-scatter.8
  172.7 10.9 all-gather.14
  187.2 61.9 all-gather.12
  251.2 8.4 all-gather.10
  276.5 10.2 reduce-scatter.12
  289.0 10.2 reduce-scatter.10
  304.8 10.9 all-gather.16
  357.4 131.5 reduce-scatter.20
  491.9 8.2 reduce-scatter.14
  505.6 127.1 reduce-scatter.22
  638.8 122.5 reduce-scatter.18
  767.7 132.7 reduce-scatter.16
